TPU v7x, 32 devices: a whole 2x2x4 slice. The times are simulated.
32 devices in a mesh: group: 2 (over y), expert: 4 (over x, core), blk: 4 (over z).
Axes of the slice: x: 2, y: 2, z: 4, core: 2. Of those that a mesh axis runs over, the one named last changes fastest.
Arguments:
- tokens: bfloat16 [128, 2048], P(('group', 'expert', 'blk')), parts along dimension 0, may hold values from -6 to 6
- route_ids: int32 [128, 2], P(('group', 'expert', 'blk')), parts along dimension 0, may hold values from 0 to 3, as said below
- route_slots: int32 [128, 2], P(('group', 'expert', 'blk')), parts along dimension 0, may hold values from 0 to 3, as said below
- gate_fixed: int32 [128, 2], P(('group', 'expert', 'blk')), parts along dimension 0, may hold values from 1 to 255
- w_gate: bfloat16 [4, 2048, 8192], P('expert', None, 'blk'), may hold values from -0.125 to 0.125
- w_up: bfloat16 [4, 2048, 8192], P('expert', None, 'blk'), may hold values from -0.125 to 0.125
- w_down: bfloat16 [4, 8192, 2048], P('expert', 'blk'), may hold values from -0.125 to 0.125
Outputs:
- mixed_out: bfloat16 [128, 2048], P(('group', 'expert', 'blk')), parts along dimension 0
There are 2 independent parts, one for each index of `group`. A program takes and returns all parts, laid end to end along the dimension named above; an argument that names none is the same for every part. Nothing has to cross between parts.
Inputs may be any that keep to these rules, and one draw needn't show every extreme that they name: `route_ids`: each row names two different experts. Among the rows of one device no expert is named more than 4 times, and one expert, the same for every device of a part, is named exactly 4 times by the rows of every device. `route_slots`: among the rows of one device, the choices that name the same expert have distinct slots.
All inputs are finite; a program needn't handle non-finite values.
Results may differ from a plain program's by a relative error of at most 0.0049.
Values may be sent and summed in bfloat16 or wider, within the bound.
A program may use at most 64 MiB of HBM per device.

v0:
```python
import jax
import jax.numpy as jnp
from jax import lax
from jax.sharding import PartitionSpec as P


def normalized(fixed_weights):
    values = fixed_weights.astype(jnp.float32)
    return values / jnp.sum(values, axis=1, keepdims=True)


def on_device(tokens, route_ids, route_slots, gate_fixed, w_gate, w_up, w_down):
    count_tok, width = tokens.shape
    experts = lax.axis_size("expert")
    capacity = 4 * count_tok // experts
    slots_all = experts * capacity
    destination_expert = route_ids * capacity + route_slots
    slot_lanes = jnp.arange(slots_all, dtype=jnp.int32)
    one_hot = (destination_expert[None, :, 0] == slot_lanes[:, None]) | (
        destination_expert[None, :, 1] == slot_lanes[:, None]
    )
    outgoing = jnp.dot(one_hot.astype(jnp.bfloat16), tokens, preferred_element_type=jnp.float32)
    outgoing = outgoing.astype(jnp.bfloat16).reshape(experts, capacity, width)
    arrived = lax.all_to_all(outgoing, "expert", split_axis=0, concat_axis=0, tiled=True).reshape(
        slots_all, width
    )
    gate_mat = w_gate[0]
    up_mat = w_up[0]
    down_mat = w_down[0]
    gathered = lax.all_gather(arrived, "blk", axis=0, tiled=True)
    gate_part = jnp.dot(gathered, gate_mat, preferred_element_type=jnp.float32)
    up_part = jnp.dot(gathered, up_mat, preferred_element_type=jnp.float32)
    hidden = (jax.nn.silu(gate_part) * up_part).astype(jnp.bfloat16)
    summed = lax.psum_scatter(
        jnp.dot(hidden, down_mat, preferred_element_type=jnp.float32),
        "blk",
        scatter_dimension=0,
        tiled=True,
    )
    returned = lax.all_to_all(
        summed.reshape(experts, capacity, width), "expert", split_axis=0, concat_axis=0, tiled=True
    )
    returned = returned.reshape(slots_all, width)
    shares = normalized(gate_fixed)
    first_pick = jnp.take(returned, destination_expert[:, 0], axis=0)
    second = jnp.take(returned, destination_expert[:, 1], axis=0)
    mixed_out = shares[:, 0:1] * first_pick + shares[:, 1:2] * second
    return mixed_out.astype(jnp.bfloat16)


def solution(mesh):
    return jax.shard_map(
        on_device,
        mesh=mesh,
        in_specs=(
            P(("group", "expert", "blk"), None),
            P(("group", "expert", "blk"), None),
            P(("group", "expert", "blk"), None),
            P(("group", "expert", "blk"), None),
            P("expert", None, "blk"),
            P("expert", None, "blk"),
            P("expert", "blk", None),
        ),
        out_specs=P(("group", "expert", "blk"), None),
        check_vma=False,
    )
```

profile of v0, /device:TPU:0, one launch (start us, length us, event | category | flops | bytes accessed | tf_op | source)
XLA Modules:
  0.0 85.0 jit_solution(3406159153187408253)
XLA Ops:
  6.5 0.0 copy-start
  6.5 0.0 reduce-scatter.2.cloned.1.call-start
  6.5 0.7 multiply_add_fusion
  7.3 0.0 copy-done
  7.3 0.1 convolution_convert_fusion
  7.4 8.1 %all_to_all.10 = bf16[4,4,2048]{2,1,0:T(4,128)(2,1)S(1)} all-to-all(bf16[4,4,2048]{2,1,0:T(4,128)(2,1)S(1)} %reshape.20), channel_id=1, replica_groups=mesh['group'=2,'expert'=4,'blk'=4] {'expert'}, dimensions={0} | all-to-all | bytes 131072 | tf_op jit(solution)/shard_map/all_to_all | solution.py:24
  15.6 14.1 %all_gather.3 = bf16[64,2048]{1,0:T(8,128)(2,1)S(1)} all-gather(bf16[16,2048]{1,0:T(8,128)(2,1)S(1)} %reshape.21), channel_id=1, replica_groups=mesh['group'=2,'expert'=4,'blk'=4] {'blk'}, dimensions={0}, use_global_device_ids=true | all-gather | bytes 327680 | tf_op jit(solution)/shard_map/all_gather | solution.py:30
  29.7 4.9 %fusion.4 = f32[64,2048]{1,0:T(8,128)S(1)} fusion(bf16[64,2048]{1,0:T(8,128)(2,1)S(1)} %all_gather.3, bf16[1,2048,2048]{2,1,0:T(8,128)(2,1)} %param.13), kind=kOutput, calls=%fused_computation.6 | convolution fusion | flops 536870912 | bytes 9175040 | tf_op jit(solution)/shard_map/dot_general | solution.py:31
  34.7 0.0 copy-start.1
  34.7 9.6 %fusion = f32[64,2048]{1,0:T(8,128)} fusion(bf16[1,2048,2048]{2,1,0:T(8,128)(2,1)} %param.15, bf16[64,2048]{1,0:T(8,128)(2,1)S(1)} %all_gather.3, bf16[1,2048,2048]{2,1,0:T(8,128)(2,1)} %param.14, f32[64,2048]{1,0:T(8,128)S(1)} %fusion.4), kind=kOutput, calls=%fused_computation.2 | convolution fusion | flops 1074528256 | bytes 18087936 | tf_op jit(solution)/shard_map/dot_general | solution.py:35
  44.3 0.0 reduce-scatter.2.cloned.1.call-update
  44.3 0.0 copy-done.1
  44.4 22.4 %reduce-scatter.2.cloned.1.call-done = f32[16,2048]{1,0:T(8,128)} async-done(((f32[64,2048]{1,0:T(8,128)}), f32[16,2048]{1,0:T(8,128)}) %reduce-scatter.2.cloned.1.call-update) | async-done | bytes 131088 | tf_op jit(solution)/shard_map/reduce_scatter | solution.py:34
  66.8 1.6 %reshape.22 = f32[4,4,2048]{2,1,0:T(4,128)} reshape(f32[16,2048]{1,0:T(8,128)} %reduce-scatter.2.cloned.1.call-done) | data formatting | bytes 262144 | tf_op jit(solution)/shard_map/reshape | solution.py:41
  68.3 3.3 %all-to-all-start.1 = ((f32[4,4,2048]{2,1,0:T(4,128)}), f32[4,4,2048]{2,1,0:T(4,128)S(1)}, u32[]{:S(2)}, u32[]{:S(2)}) async-start(f32[4,4,2048]{2,1,0:T(4,128)} %reshape.22), calls=%async_computation.2 | async-start | bytes 262144 | tf_op jit(solution)/shard_map/all_to_all | solution.py:40
  71.7 4.6 %all-to-all-done.1 = f32[4,4,2048]{2,1,0:T(4,128)S(1)} async-done(((f32[4,4,2048]{2,1,0:T(4,128)}), f32[4,4,2048]{2,1,0:T(4,128)S(1)}, u32[]{:S(2)}, u32[]{:S(2)}) %all-to-all-start.1) | async-done | bytes 131104 | tf_op jit(solution)/shard_map/all_to_all | solution.py:40
  76.3 0.6 gather_fusion
  76.9 0.6 gather_fusion.1
  77.5 0.7 fusion.21
  (9 shorter events, 0.2 us)
Async XLA Ops:
  6.5 0.7 copy-start
  6.5 60.2 %reduce-scatter.2.cloned.1.call-start = ((), (), s32[]{:S(2)}) async-start(), calls=%async_computation.3 | async-start | bytes 655360 | tf_op jit(solution)/shard_map/reduce_scatter | solution.py:34
  34.7 9.6 %copy-start.1 = (s32[4,2]{0,1:T(2,128)S(1)}, s32[4,2]{0,1:T(2,128)}, u32[]{:S(2)}) copy-start(s32[4,2]{0,1:T(2,128)} %param.12) | copy-start | bytes 100
  68.3 7.9 %all-to-all-start.1 = ((f32[4,4,2048]{2,1,0:T(4,128)}), f32[4,4,2048]{2,1,0:T(4,128)S(1)}, u32[]{:S(2)}, u32[]{:S(2)}) async-start(f32[4,4,2048]{2,1,0:T(4,128)} %reshape.22), calls=%async_computation.2 | async-start | bytes 262144 | tf_op jit(solution)/shard_map/all_to_all | solution.py:40
Sparse Core Ops, SparseCore 0:
  44.4 22.2 reduce-scatter.1
where the time goes:
time: 85.4 us; the launch traced here: 85 us
  waiting for transfers between devices  27 us (32%)
  blocking collectives  22.3 us (26%)
  matrix products  14.7 us (17%)
  between operations  13.5 us (16%)
  starting transfers between devices  3.32 us (4%)
  local copies, waits for them, and re-layouts  2.86 us (3%)
  other arithmetic  1.45 us (2%)
    reduce_scatter x1, waiting for transfers between devices, on_device(): lax.psum_scatter(jnp.dot(hidden, down_mat, preferred_element_type=jnp.flo...  22.4 us
    all_gather x1, blocking collectives, on_device(): gathered = lax.all_gather(arrived, 'blk', axis=0, tiled=True)  14.1 us
    dot_general x1, matrix products, on_device(): jnp.dot(hidden, down_mat, preferred_element_type=jnp.float32)  9.6 us
    all_to_all x1, blocking collectives, on_device(): lax.all_to_all(outgoing, 'expert', split_axis=0, concat_axis=0, tiled=True)  8.13 us
    dot_general x1, matrix products, on_device(): gate_part = jnp.dot(gathered, gate_mat, preferred_element_type=jnp.float32)  4.94 us
    all_to_all x1, waiting for transfers between devices, on_device(): lax.all_to_all(summed.reshape(experts, capacity, width), 'expert', split_...  4.58 us
    all_to_all x1, starting transfers between devices, on_device(): lax.all_to_all(summed.reshape(experts, capacity, width), 'expert', split_...  3.32 us
  transfers between devices with their start and end apart: 2, of which 2 were waited for; matrix products, arithmetic and copies ran while one was open for 0% of the time, Pallas kernels for 0%

commit v1 on v0

--- a/solution.py
+++ b/solution.py
@@ -1,7 +1,15 @@
+import functools
+
 import jax
 import jax.numpy as jnp
 from jax import lax
+from jax.experimental import pallas as pl
+from jax.experimental.pallas import tpu as pltpu
 from jax.sharding import PartitionSpec as P
+
+MESH = pl.DeviceIdType.MESH
+CHUNKS = 4
+LANES = 128
 
 
 def normalized(fixed_weights):
@@ -9,7 +17,7 @@
     return values / jnp.sum(values, axis=1, keepdims=True)
 
 
-def on_device(tokens, route_ids, route_slots, gate_fixed, w_gate, w_up, w_down):
+def routed(tokens, route_ids, route_slots, gate_fixed, w_gate, w_up, w_down):
     count_tok, width = tokens.shape
     experts = lax.axis_size("expert")
     capacity = 4 * count_tok // experts
@@ -24,15 +32,12 @@
     arrived = lax.all_to_all(outgoing, "expert", split_axis=0, concat_axis=0, tiled=True).reshape(
         slots_all, width
     )
-    gate_mat = w_gate[0]
-    up_mat = w_up[0]
-    down_mat = w_down[0]
     gathered = lax.all_gather(arrived, "blk", axis=0, tiled=True)
-    gate_part = jnp.dot(gathered, gate_mat, preferred_element_type=jnp.float32)
-    up_part = jnp.dot(gathered, up_mat, preferred_element_type=jnp.float32)
+    gate_part = jnp.dot(gathered, w_gate[0], preferred_element_type=jnp.float32)
+    up_part = jnp.dot(gathered, w_up[0], preferred_element_type=jnp.float32)
     hidden = (jax.nn.silu(gate_part) * up_part).astype(jnp.bfloat16)
     summed = lax.psum_scatter(
-        jnp.dot(hidden, down_mat, preferred_element_type=jnp.float32),
+        jnp.dot(hidden, w_down[0], preferred_element_type=jnp.float32),
         "blk",
         scatter_dimension=0,
         tiled=True,
@@ -48,6 +53,226 @@
     return mixed_out.astype(jnp.bfloat16)
 
 
+def kernel(
+    experts, blks, tok_ref, ids_ref, gate_ref, wg_hbm, wu_hbm, wd_hbm, out_ref,
+    wg, wu, wd, rows_in, rows_f32, rows, hidden, part, part_sib, back, back_in,
+    w_sem, tok_send, tok_fwd, tok_recv, sib_send, sib_recv, back_send, back_recv,
+):
+    count_tok, width = tok_ref.shape
+    peers = experts // 2 * blks
+    half = peers * count_tok
+    chunks_ff, unused, cols_ff = wg.shape
+    chunks, unused, cols = wd.shape
+    expert, blk = lax.axis_index("expert"), lax.axis_index("blk")
+    core = lax.rem(expert, 2)
+    place = expert // 2 * blks + blk
+    sibling = {"expert": expert + 1 - 2 * core, "blk": blk}
+
+    def peer_at(at):
+        return {"expert": at // blks * 2 + core, "blk": lax.rem(at, blks)}
+
+    def weight_copy(mat, c):
+        hbm, vmem = ((wg_hbm, wg), (wu_hbm, wu), (wd_hbm, wd))[mat]
+        n = vmem.shape[2]
+        return pltpu.make_async_copy(
+            hbm.at[0, :, pl.ds(pl.multiple_of(c * n, n), n)], vmem.at[c], w_sem.at[mat, c]
+        )
+
+    for c in range(chunks_ff):
+        weight_copy(0, c).start()
+        weight_copy(1, c).start()
+    for c in range(chunks):
+        weight_copy(2, c).start()
+
+    barrier = pltpu.get_barrier_semaphore()
+    pl.semaphore_signal(barrier, inc=1, device_id=sibling, device_id_type=MESH)
+    for j in range(1, peers):
+        pl.semaphore_signal(
+            barrier, inc=1, device_id=peer_at(lax.rem(place + j, peers)), device_id_type=MESH
+        )
+
+    lane = lax.broadcasted_iota(jnp.int32, (count_tok, LANES), 1)
+    marks = jnp.where(lane == ids_ref[:, 0:1], gate_ref[:, 0:1], 0)
+    marks = marks + jnp.where(lane == ids_ref[:, 1:2], gate_ref[:, 1:2], 0)
+    rows_in[core, place, :, 0:width] = tok_ref[...]
+    rows_in[core, place, :, width : width + LANES] = marks.astype(jnp.float32).astype(jnp.bfloat16)
+
+    pl.semaphore_wait(barrier, peers)
+
+    def to_peer(j):
+        return pltpu.make_async_remote_copy(
+            src_ref=rows_in.at[core, place],
+            dst_ref=rows_in.at[core, place],
+            send_sem=tok_send.at[j],
+            recv_sem=tok_recv.at[core, place],
+            device_id=peer_at(lax.rem(place + j, peers)),
+            device_id_type=MESH,
+        )
+
+    def arrival(side, at):
+        return pltpu.make_async_remote_copy(
+            src_ref=rows_in.at[side, at],
+            dst_ref=rows_in.at[side, at],
+            send_sem=tok_fwd.at[at],
+            recv_sem=tok_recv.at[side, at],
+            device_id=sibling,
+            device_id_type=MESH,
+        )
+
+    for j in range(1, peers):
+        to_peer(j).start()
+    arrival(core, place).start()
+    for j in range(1, peers):
+        at = lax.rem(place + peers - j, peers)
+        arrival(core, at).wait_recv()
+        arrival(core, at).start()
+    for j in range(peers):
+        arrival(1 - core, j).wait_recv()
+
+    for side in range(2):
+        for at in range(peers):
+            first = (side * peers + at) * count_tok
+            rows_f32[first : first + count_tok, :] = rows_in[side, at].astype(jnp.float32)
+    rows[...] = rows_f32[:, 0:width].astype(jnp.bfloat16)
+    marks = rows_f32[:, width : width + LANES]
+    lane = lax.broadcasted_iota(jnp.int32, marks.shape, 1)
+    share = jnp.sum(jnp.where(lane == expert, marks, 0.0), axis=1, keepdims=True)
+    share = share / jnp.sum(marks, axis=1, keepdims=True)
+
+    def up_step(c, carry):
+        weight_copy(0, c).wait()
+        gate_part = jnp.dot(rows[...], wg[c], preferred_element_type=jnp.float32)
+        weight_copy(1, c).wait()
+        up_part = jnp.dot(rows[...], wu[c], preferred_element_type=jnp.float32)
+        value = gate_part / (1.0 + jnp.exp(-gate_part)) * up_part
+        hidden[:, pl.ds(pl.multiple_of(c * cols_ff, cols_ff), cols_ff)] = value.astype(jnp.bfloat16)
+        return carry
+
+    lax.fori_loop(0, chunks_ff, up_step, 0)
+
+    def pair(c):
+        mine = pl.multiple_of(core * half, half)
+        other = pl.multiple_of((1 - core) * half, half)
+        return mine, pltpu.make_async_remote_copy(
+            src_ref=part.at[c, pl.ds(other, half), :],
+            dst_ref=part_sib.at[c],
+            send_sem=sib_send.at[c],
+            recv_sem=sib_recv.at[c],
+            device_id=sibling,
+            device_id_type=MESH,
+        )
+
+    def home(c, j):
+        at = lax.rem(place + j, peers)
+        return pltpu.make_async_remote_copy(
+            src_ref=back.at[c, at],
+            dst_ref=back_in.at[c, place],
+            send_sem=back_send.at[c, j],
+            recv_sem=back_recv.at[c, place],
+            device_id=peer_at(at),
+            device_id_type=MESH,
+        )
+
+    def from_peer(c, j):
+        at = lax.rem(place + peers - j, peers)
+        return pltpu.make_async_remote_copy(
+            src_ref=back.at[c, at],
+            dst_ref=back_in.at[c, at],
+            send_sem=back_send.at[c, j],
+            recv_sem=back_recv.at[c, at],
+            device_id=peer_at(at),
+            device_id_type=MESH,
+        )
+
+    def send_home(c):
+        mine, copy = pair(c)
+        copy.wait_recv()
+        both = part[c, pl.ds(mine, half), :] + part_sib[c]
+        for at in range(peers):
+            back[c, at] = both[at * count_tok : (at + 1) * count_tok, :].astype(jnp.bfloat16)
+        for j in range(1, peers):
+            home(c, j).start()
+
+    for c in range(chunks):
+        weight_copy(2, c).wait()
+        part[c] = jnp.dot(hidden[...], wd[c], preferred_element_type=jnp.float32) * share
+        pair(c)[1].start()
+        if c > 0:
+            send_home(c - 1)
+    send_home(chunks - 1)
+
+    for c in range(chunks):
+        total = back[c, place].astype(jnp.float32)
+        for j in range(1, peers):
+            from_peer(c, j).wait_recv()
+            total = total + back_in[c, lax.rem(place + peers - j, peers)].astype(jnp.float32)
+        out_ref[:, c * cols : (c + 1) * cols] = total.astype(jnp.bfloat16)
+
+    arrival(core, place).wait_send()
+    for j in range(1, peers):
+        to_peer(j).wait_send()
+        arrival(core, lax.rem(place + peers - j, peers)).wait_send()
+    for c in range(chunks):
+        pair(c)[1].wait_send()
+        for j in range(1, peers):
+            home(c, j).wait_send()
+
+
+def dense(tokens, route_ids, route_slots, gate_fixed, w_gate, w_up, w_down):
+    count_tok, width = tokens.shape
+    units = w_gate.shape[2]
+    experts, blks = lax.axis_size("expert"), lax.axis_size("blk")
+    peers = experts // 2 * blks
+    half = peers * count_tok
+    rows_all = 2 * half
+    cols, cols_ff = width // CHUNKS, units // CHUNKS
+    f32, bf16 = jnp.float32, jnp.bfloat16
+    dma = pltpu.SemaphoreType.DMA
+    return pl.pallas_call(
+        functools.partial(kernel, experts, blks),
+        out_shape=jax.ShapeDtypeStruct((count_tok, width), bf16),
+        in_specs=[pl.BlockSpec(memory_space=pltpu.VMEM)] * 3
+        + [pl.BlockSpec(memory_space=pl.ANY)] * 3,
+        out_specs=pl.BlockSpec(memory_space=pltpu.VMEM),
+        scratch_shapes=[
+            pltpu.VMEM((CHUNKS, width, cols_ff), bf16),
+            pltpu.VMEM((CHUNKS, width, cols_ff), bf16),
+            pltpu.VMEM((CHUNKS, units, cols), bf16),
+            pltpu.VMEM((2, peers, count_tok, width + LANES), bf16),
+            pltpu.VMEM((rows_all, width + LANES), f32),
+            pltpu.VMEM((rows_all, width), bf16),
+            pltpu.VMEM((rows_all, units), bf16),
+            pltpu.VMEM((CHUNKS, rows_all, cols), f32),
+            pltpu.VMEM((CHUNKS, half, cols), f32),
+            pltpu.VMEM((CHUNKS, peers, count_tok, cols), bf16),
+            pltpu.VMEM((CHUNKS, peers, count_tok, cols), bf16),
+            dma((3, CHUNKS)),
+            dma((peers,)),
+            dma((peers,)),
+            dma((2, peers)),
+            dma((CHUNKS,)),
+            dma((CHUNKS,)),
+            dma((CHUNKS, peers)),
+            dma((CHUNKS, peers)),
+        ],
+        compiler_params=pltpu.CompilerParams(
+            collective_id=0, has_side_effects=True, vmem_limit_bytes=48 * 1024 * 1024
+        ),
+        cost_estimate=pl.CostEstimate(
+            flops=6 * rows_all * width * units,
+            bytes_accessed=6 * width * units,
+            transcendentals=rows_all * units,
+        ),
+    )(tokens, route_ids, gate_fixed, w_gate, w_up, w_down)
+
+
+def on_device(tokens, *others):
+    count_tok = tokens.shape[0]
+    experts = lax.axis_size("expert")
+    whole = 4 * count_tok // experts >= count_tok and experts % 2 == 0 and experts <= LANES
+    return (dense if whole else routed)(tokens, *others)
+
+
 def solution(mesh):
     return jax.shard_map(
         on_device,

time: 85.4 us -> 27.4 us (0.32)
  waiting for transfers between devices: 27 us -> 0 us
  Pallas kernels: 0 us -> 24.3 us
  blocking collectives: 22.3 us -> 0 us
  matrix products: 14.7 us -> 0 us
  between operations: 13.5 us -> 0.01 us
  starting transfers between devices: 3.32 us -> 0 us
  other arithmetic: 1.45 us -> 0 us
    pallas_call x0 -> x1, Pallas kernels: none -> 24.3 us  [dense(): pl.pallas_call(functools.partial(kernel, experts, blks), out_shape=jax.Sh...]
    reduce_scatter x1 -> x0, waiting for transfers between devices: 22.4 us -> none  [on_device(): lax.psum_scatter(jnp.dot(hidden, down_mat, preferred_element_type=jnp.flo...]
    dot_general x3 -> x0, matrix products: 14.7 us -> none  [the longest x1 9.6 us: on_device(): jnp.dot(hidden, down_mat, preferred_element_type=jnp.float32)]
    all_gather x1 -> x0, blocking collectives: 14.1 us -> none  [on_device(): gathered = lax.all_gather(arrived, 'blk', axis=0, tiled=True)]
    all_to_all x1 -> x0, blocking collectives: 8.13 us -> none  [on_device(): lax.all_to_all(outgoing, 'expert', split_axis=0, concat_axis=0, tiled=True)]
    all_to_all x1 -> x0, waiting for transfers between devices: 4.58 us -> none  [on_device(): lax.all_to_all(summed.reshape(experts, capacity, width), 'expert', split_...]
    all_to_all x1 -> x0, starting transfers between devices: 3.32 us -> none  [on_device(): lax.all_to_all(summed.reshape(experts, capacity, width), 'expert', split_...]
    unnamed x4 -> x5, local copies, waits for them, and re-layouts: 0.01 us -> 2.85 us
  transfers between devices with their start and end apart: 2 -> 0, of which waited for: 2 -> 0; matrix products, arithmetic and copies ran while one was open for 0% -> 0% of each run, Pallas kernels for 0% -> 0%
where the time goes in v1:
time: 27.4 us; the launch traced here: 27.2 us
  Pallas kernels  24.3 us (89%)
  local copies, waits for them, and re-layouts  2.85 us (10%)
    pallas_call x1, Pallas kernels, dense(): pl.pallas_call(functools.partial(kernel, experts, blks), out_shape=jax.Sh...  24.3 us
    unnamed x5, local copies, waits for them, and re-layouts  2.85 us

profile of v1, /device:TPU:0, one launch (start us, length us, event | category | flops | bytes accessed | tf_op | source)
XLA Modules:
  0.0 27.2 jit_solution(16061553856040895196)
XLA Ops:
  0.0 0.8 %copy.7.ids_ref = s32[4,2]{1,0:T(4,128)S(1)} copy(s32[4,2]{0,1:T(2,128)} %param.8) | data formatting | bytes 64 | tf_op args[1]
  0.8 0.8 %copy.8.gate_ref = s32[4,2]{1,0:T(4,128)S(1)} copy(s32[4,2]{0,1:T(2,128)} %param.9) | data formatting | bytes 64 | tf_op args[3]
  1.5 0.0 copy-start
  1.5 0.7 %copy-done = bf16[4,2048]{1,0:T(4,128)(2,1)S(1)} copy-done((bf16[4,2048]{1,0:T(4,128)(2,1)S(1)}, bf16[4,2048]{1,0:T(4,128)(2,1)}, u32[]{:S(2)}) %copy-start) | copy-done | bytes 16408
  2.2 24.3 %shard_map.64 = bf16[4,2048]{1,0:T(4,128)(2,1)S(1)} custom-call(bf16[4,2048]{1,0:T(4,128)(2,1)S(1)} %copy-done, s32[4,2]{1,0:T(4,128)S(1)} %copy.7.ids_ref, s32[4,2]{1,0:T(4,128)S(1)} %copy.8.gate_ref, bf16[1,2048,2048]{2,1,0:T(8,128)(2,1)} %wg_hbm.1, bf16[1,2048,2048]{2,1,0:T(8,128)(2,1)} %wu_hbm.1, bf16[1,2048,2048]{2,1,0:T(8,128)(2,1)} %wd_hbm.1), custom_call_target="tpu_custom_call" | custom-call | flops 1610612736 | bytes 25165824 | tf_op jit(solution)/shard_map/pallas_call | solution.py:231
  26.6 0.6 %copy.10 = bf16[4,2048]{1,0:T(4,128)(2,1)} copy(bf16[4,2048]{1,0:T(4,128)(2,1)S(1)} %shard_map.64) | data formatting | bytes 32768
Async XLA Ops:
  1.5 0.7 %copy-start = (bf16[4,2048]{1,0:T(4,128)(2,1)S(1)}, bf16[4,2048]{1,0:T(4,128)(2,1)}, u32[]{:S(2)}) copy-start(bf16[4,2048]{1,0:T(4,128)(2,1)} %tok_ref.1) | copy-start | bytes 49156

commit v2 on v1

--- a/solution.py
+++ b/solution.py
@@ -54,12 +54,13 @@
 
 
 def kernel(
-    experts, blks, tok_ref, ids_ref, gate_ref, wg_hbm, wu_hbm, wd_hbm, out_ref,
-    wg, wu, wd, rows_in, rows_f32, rows, hidden, part, part_sib, back, back_in,
-    w_sem, tok_send, tok_fwd, tok_recv, sib_send, sib_recv, back_send, back_recv,
+    experts, blks, tok_hbm, ids_hbm, gate_hbm, wg_hbm, wu_hbm, wd_hbm, out_ref,
+    ids, gates, wg, wu, wd, rows_in, rows_f32, rows, hidden, part, part_sib, back, back_in,
+    in_sem, w_sem, tok_send, tok_fwd, tok_recv, sib_send, sib_recv, back_send, back_recv,
 ):
-    count_tok, width = tok_ref.shape
-    peers = experts // 2 * blks
+    count_tok, width = tok_hbm.shape
+    across = experts // 2
+    peers = across * blks
     half = peers * count_tok
     chunks_ff, unused, cols_ff = wg.shape
     chunks, unused, cols = wd.shape
@@ -68,6 +69,19 @@
     place = expert // 2 * blks + blk
     sibling = {"expert": expert + 1 - 2 * core, "blk": blk}
 
+    steps = sorted(
+        [(dx, dz) for dx in range(across) for dz in range(blks) if dx or dz],
+        key=lambda d: -2 * min(d[1], blks - d[1]) - min(d[0], across - d[0]),
+    )
+
+    def ahead(j):
+        dx, dz = steps[j]
+        return lax.rem(expert // 2 + dx, across) * blks + lax.rem(blk + dz, blks)
+
+    def behind(j):
+        dx, dz = steps[j]
+        return lax.rem(expert // 2 + across - dx, across) * blks + lax.rem(blk + blks - dz, blks)
+
     def peer_at(at):
         return {"expert": at // blks * 2 + core, "blk": lax.rem(at, blks)}
 
@@ -78,24 +92,41 @@
             hbm.at[0, :, pl.ds(pl.multiple_of(c * n, n), n)], vmem.at[c], w_sem.at[mat, c]
         )
 
-    for c in range(chunks_ff):
+    own = [
+        pltpu.make_async_copy(ids_hbm, ids, in_sem.at[0]),
+        pltpu.make_async_copy(gate_hbm, gates, in_sem.at[1]),
+        pltpu.make_async_copy(
+            tok_hbm, rows_in.at[core, place, :, pl.ds(0, width)], in_sem.at[2]
+        ),
+    ]
+    for copy in own:
+        copy.start()
+    for c in range(chunks_ff // 2):
         weight_copy(0, c).start()
         weight_copy(1, c).start()
-    for c in range(chunks):
-        weight_copy(2, c).start()
 
     barrier = pltpu.get_barrier_semaphore()
     pl.semaphore_signal(barrier, inc=1, device_id=sibling, device_id_type=MESH)
-    for j in range(1, peers):
+    for j in range(peers - 1):
         pl.semaphore_signal(
-            barrier, inc=1, device_id=peer_at(lax.rem(place + j, peers)), device_id_type=MESH
-        )
-
-    lane = lax.broadcasted_iota(jnp.int32, (count_tok, LANES), 1)
-    marks = jnp.where(lane == ids_ref[:, 0:1], gate_ref[:, 0:1], 0)
-    marks = marks + jnp.where(lane == ids_ref[:, 1:2], gate_ref[:, 1:2], 0)
-    rows_in[core, place, :, 0:width] = tok_ref[...]
-    rows_in[core, place, :, width : width + LANES] = marks.astype(jnp.float32).astype(jnp.bfloat16)
+            barrier, inc=1, device_id=peer_at(ahead(j)), device_id_type=MESH
+        )
+
+    for copy in own:
+        copy.wait()
+    square = (count_tok, count_tok)
+    diagonal = lax.broadcasted_iota(jnp.int32, square, 0) == lax.broadcasted_iota(
+        jnp.int32, square, 1
+    )
+
+    def column(ref, k):
+        line = jnp.broadcast_to(ref[k : k + 1, :].astype(jnp.float32), square)
+        return jnp.sum(jnp.where(diagonal, line, 0.0), axis=1, keepdims=True)
+
+    lane = lax.broadcasted_iota(jnp.int32, (count_tok, LANES), 1).astype(jnp.float32)
+    marks = jnp.where(lane == column(ids, 0), column(gates, 0), 0.0)
+    marks = marks + jnp.where(lane == column(ids, 1), column(gates, 1), 0.0)
+    rows_in[core, place, :, width : width + LANES] = marks.astype(jnp.bfloat16)
 
     pl.semaphore_wait(barrier, peers)
 
@@ -105,7 +136,7 @@
             dst_ref=rows_in.at[core, place],
             send_sem=tok_send.at[j],
             recv_sem=tok_recv.at[core, place],
-            device_id=peer_at(lax.rem(place + j, peers)),
+            device_id=peer_at(ahead(j)),
             device_id_type=MESH,
         )
 
@@ -119,13 +150,18 @@
             device_id_type=MESH,
         )
 
-    for j in range(1, peers):
+    for j in range(peers - 1):
         to_peer(j).start()
     arrival(core, place).start()
-    for j in range(1, peers):
-        at = lax.rem(place + peers - j, peers)
+    for c in range(chunks_ff // 2, chunks_ff):
+        weight_copy(0, c).start()
+        weight_copy(1, c).start()
+    for j in reversed(range(peers - 1)):
+        at = behind(j)
         arrival(core, at).wait_recv()
         arrival(core, at).start()
+    for c in range(chunks):
+        weight_copy(2, c).start()
     for j in range(peers):
         arrival(1 - core, j).wait_recv()
 
@@ -139,16 +175,24 @@
     share = jnp.sum(jnp.where(lane == expert, marks, 0.0), axis=1, keepdims=True)
     share = share / jnp.sum(marks, axis=1, keepdims=True)
 
-    def up_step(c, carry):
+    def products(c):
         weight_copy(0, c).wait()
-        gate_part = jnp.dot(rows[...], wg[c], preferred_element_type=jnp.float32)
         weight_copy(1, c).wait()
-        up_part = jnp.dot(rows[...], wu[c], preferred_element_type=jnp.float32)
+        return (
+            jnp.dot(rows[...], wg[c], preferred_element_type=jnp.float32),
+            jnp.dot(rows[...], wu[c], preferred_element_type=jnp.float32),
+        )
+
+    def activate(c, gate_part, up_part):
         value = gate_part / (1.0 + jnp.exp(-gate_part)) * up_part
-        hidden[:, pl.ds(pl.multiple_of(c * cols_ff, cols_ff), cols_ff)] = value.astype(jnp.bfloat16)
-        return carry
-
-    lax.fori_loop(0, chunks_ff, up_step, 0)
+        hidden[:, c * cols_ff : (c + 1) * cols_ff] = value.astype(jnp.bfloat16)
+
+    held = products(0)
+    for c in range(1, chunks_ff):
+        following = products(c)
+        activate(c - 1, *held)
+        held = following
+    activate(chunks_ff - 1, *held)
 
     def pair(c):
         mine = pl.multiple_of(core * half, half)
@@ -163,7 +207,7 @@
         )
 
     def home(c, j):
-        at = lax.rem(place + j, peers)
+        at = ahead(j)
         return pltpu.make_async_remote_copy(
             src_ref=back.at[c, at],
             dst_ref=back_in.at[c, place],
@@ -174,7 +218,7 @@
         )
 
     def from_peer(c, j):
-        at = lax.rem(place + peers - j, peers)
+        at = behind(j)
         return pltpu.make_async_remote_copy(
             src_ref=back.at[c, at],
             dst_ref=back_in.at[c, at],
@@ -190,7 +234,7 @@
         both = part[c, pl.ds(mine, half), :] + part_sib[c]
         for at in range(peers):
             back[c, at] = both[at * count_tok : (at + 1) * count_tok, :].astype(jnp.bfloat16)
-        for j in range(1, peers):
+        for j in range(peers - 1):
             home(c, j).start()
 
     for c in range(chunks):
@@ -203,18 +247,18 @@
 
     for c in range(chunks):
         total = back[c, place].astype(jnp.float32)
-        for j in range(1, peers):
+        for j in range(peers - 1):
             from_peer(c, j).wait_recv()
-            total = total + back_in[c, lax.rem(place + peers - j, peers)].astype(jnp.float32)
+            total = total + back_in[c, behind(j)].astype(jnp.float32)
         out_ref[:, c * cols : (c + 1) * cols] = total.astype(jnp.bfloat16)
 
     arrival(core, place).wait_send()
-    for j in range(1, peers):
+    for j in range(peers - 1):
         to_peer(j).wait_send()
-        arrival(core, lax.rem(place + peers - j, peers)).wait_send()
+        arrival(core, behind(j)).wait_send()
     for c in range(chunks):
         pair(c)[1].wait_send()
-        for j in range(1, peers):
+        for j in range(peers - 1):
             home(c, j).wait_send()
 
 
@@ -231,10 +275,11 @@
     return pl.pallas_call(
         functools.partial(kernel, experts, blks),
         out_shape=jax.ShapeDtypeStruct((count_tok, width), bf16),
-        in_specs=[pl.BlockSpec(memory_space=pltpu.VMEM)] * 3
-        + [pl.BlockSpec(memory_space=pl.ANY)] * 3,
+        in_specs=[pl.BlockSpec(memory_space=pltpu.HBM)] * 6,
         out_specs=pl.BlockSpec(memory_space=pltpu.VMEM),
         scratch_shapes=[
+            pltpu.VMEM((2, count_tok), jnp.int32),
+            pltpu.VMEM((2, count_tok), jnp.int32),
             pltpu.VMEM((CHUNKS, width, cols_ff), bf16),
             pltpu.VMEM((CHUNKS, width, cols_ff), bf16),
             pltpu.VMEM((CHUNKS, units, cols), bf16),
@@ -246,6 +291,7 @@
             pltpu.VMEM((CHUNKS, half, cols), f32),
             pltpu.VMEM((CHUNKS, peers, count_tok, cols), bf16),
             pltpu.VMEM((CHUNKS, peers, count_tok, cols), bf16),
+            dma((3,)),
             dma((3, CHUNKS)),
             dma((peers,)),
             dma((peers,)),
@@ -256,14 +302,14 @@
             dma((CHUNKS, peers)),
         ],
         compiler_params=pltpu.CompilerParams(
-            collective_id=0, has_side_effects=True, vmem_limit_bytes=48 * 1024 * 1024
+            collective_id=0, has_side_effects=True, vmem_limit_bytes=63 * 1024 * 1024
         ),
         cost_estimate=pl.CostEstimate(
             flops=6 * rows_all * width * units,
             bytes_accessed=6 * width * units,
             transcendentals=rows_all * units,
         ),
-    )(tokens, route_ids, gate_fixed, w_gate, w_up, w_down)
+    )(tokens, route_ids.T, gate_fixed.T, w_gate, w_up, w_down)
 
 
 def on_device(tokens, *others):

time: 27.4 us -> 26 us (0.949)
  local copies, waits for them, and re-layouts: 2.85 us -> 1.33 us
    unnamed x5 -> x1, local copies, waits for them, and re-layouts: 2.85 us -> 1.33 us
where the time goes in v2:
time: 26 us; the launch traced here: 25.6 us
  Pallas kernels  24.3 us (93%)
  local copies, waits for them, and re-layouts  1.33 us (5%)
    pallas_call x1, Pallas kernels, dense(): pl.pallas_call(functools.partial(kernel, experts, blks), out_shape=jax.Sh...  24.3 us
    unnamed x1, local copies, waits for them, and re-layouts  1.33 us

profile of v2, /device:TPU:0, one launch (start us, length us, event | category | flops | bytes accessed | tf_op | source)
XLA Modules:
  0.0 25.6 jit_solution(8956908225686413664)
XLA Ops:
  0.0 24.3 %shard_map.64 = bf16[4,2048]{1,0:T(4,128)(2,1)} custom-call(bf16[4,2048]{1,0:T(4,128)(2,1)} %tok_hbm.1, s32[2,4]{1,0:T(2,128)} %bitcast.2, s32[2,4]{1,0:T(2,128)} %bitcast.3, bf16[1,2048,2048]{2,1,0:T(8,128)(2,1)} %wg_hbm.1, bf16[1,2048,2048]{2,1,0:T(8,128)(2,1)} %wu_hbm.1, bf16[1,2048,2048]{2,1,0:T(8,128)(2,1)} %wd_hbm.1), custom_call_target="tpu_custom_call" | custom-call | flops 1610612736 | bytes 25165824 | tf_op jit(solution)/shard_map/pallas_call | solution.py:275
  24.3 1.3 %copy.8 = bf16[4,2048]{1,0:T(4,128)(2,1)} copy(bf16[4,2048]{1,0:T(4,128)(2,1)} %shard_map.64) | data formatting | bytes 32768

commit v3 on v2

v3 whole, which is shorter than its diff:
```python
import functools

import jax
import jax.numpy as jnp
from jax import lax
from jax.experimental import pallas as pl
from jax.experimental.pallas import tpu as pltpu
from jax.sharding import PartitionSpec as P

MESH = pl.DeviceIdType.MESH
CHUNKS = 4
CHUNKS_FF = 2
LANES = 128


def normalized(fixed_weights):
    values = fixed_weights.astype(jnp.float32)
    return values / jnp.sum(values, axis=1, keepdims=True)


def routed(tokens, route_ids, route_slots, gate_fixed, w_gate, w_up, w_down):
    count_tok, width = tokens.shape
    experts = lax.axis_size("expert")
    capacity = 4 * count_tok // experts
    slots_all = experts * capacity
    destination_expert = route_ids * capacity + route_slots
    slot_lanes = jnp.arange(slots_all, dtype=jnp.int32)
    one_hot = (destination_expert[None, :, 0] == slot_lanes[:, None]) | (
        destination_expert[None, :, 1] == slot_lanes[:, None]
    )
    outgoing = jnp.dot(one_hot.astype(jnp.bfloat16), tokens, preferred_element_type=jnp.float32)
    outgoing = outgoing.astype(jnp.bfloat16).reshape(experts, capacity, width)
    arrived = lax.all_to_all(outgoing, "expert", split_axis=0, concat_axis=0, tiled=True).reshape(
        slots_all, width
    )
    gathered = lax.all_gather(arrived, "blk", axis=0, tiled=True)
    gate_part = jnp.dot(gathered, w_gate[0], preferred_element_type=jnp.float32)
    up_part = jnp.dot(gathered, w_up[0], preferred_element_type=jnp.float32)
    hidden = (jax.nn.silu(gate_part) * up_part).astype(jnp.bfloat16)
    summed = lax.psum_scatter(
        jnp.dot(hidden, w_down[0], preferred_element_type=jnp.float32),
        "blk",
        scatter_dimension=0,
        tiled=True,
    )
    returned = lax.all_to_all(
        summed.reshape(experts, capacity, width), "expert", split_axis=0, concat_axis=0, tiled=True
    )
    returned = returned.reshape(slots_all, width)
    shares = normalized(gate_fixed)
    first_pick = jnp.take(returned, destination_expert[:, 0], axis=0)
    second = jnp.take(returned, destination_expert[:, 1], axis=0)
    mixed_out = shares[:, 0:1] * first_pick + shares[:, 1:2] * second
    return mixed_out.astype(jnp.bfloat16)


def kernel(
    groups, experts, blks, tok_hbm, ids_hbm, gate_hbm, wg_hbm, wu_hbm, wd_hbm, out_ref,
    ids, gates, wg, wu, wd, rows_in, rows_f32, rows, hidden, part, part_sib, over, over_in,
    back, back_in, in_sem, w_sem, z_send, x_send, y_send, s_send, tok_recv,
    sib_send, sib_recv, over_send, over_recv, back_send, back_recv,
):
    count_tok, width = tok_hbm.shape
    across = experts // 2
    peers = across * blks
    quarter = peers * count_tok
    half = groups * quarter
    chunks_ff, unused, cols_ff = wg.shape
    chunks, units, cols = wd.shape
    group, expert, blk = (lax.axis_index(name) for name in ("group", "expert", "blk"))
    core, row = lax.rem(expert, 2), expert // 2
    place = row * blks + blk
    sibling = {"group": group, "expert": expert + 1 - 2 * core, "blk": blk}
    facing = {"group": 1 - group, "expert": expert, "blk": blk}

    steps = sorted(
        [(dx, dz) for dx in range(across) for dz in range(blks) if dx or dz],
        key=lambda d: -2 * min(d[1], blks - d[1]) - min(d[0], across - d[0]),
    )

    def ahead(dx, dz):
        return lax.rem(row + dx, across) * blks + lax.rem(blk + dz, blks)

    def behind(dx, dz):
        return lax.rem(row + across - dx, across) * blks + lax.rem(blk + blks - dz, blks)

    def peer_at(at):
        return {"group": group, "expert": at // blks * 2 + core, "blk": lax.rem(at, blks)}

    def weight_copy(mat, c):
        first = group * units
        if mat == 2:
            src = wd_hbm.at[0, pl.ds(pl.multiple_of(first, units), units), pl.ds(c * cols, cols)]
            dst = wd.at[c]
        else:
            columns = pl.ds(pl.multiple_of(first + c * cols_ff, cols_ff), cols_ff)
            src = (wg_hbm, wu_hbm)[mat].at[0, :, columns]
            dst = (wg, wu)[mat].at[c]
        return pltpu.make_async_copy(src, dst, w_sem.at[mat, c])

    own = [
        pltpu.make_async_copy(ids_hbm, ids, in_sem.at[0]),
        pltpu.make_async_copy(gate_hbm, gates, in_sem.at[1]),
        pltpu.make_async_copy(
            tok_hbm, rows_in.at[core, group, place, :, pl.ds(0, width)], in_sem.at[2]
        ),
    ]
    for copy in own:
        copy.start()

    barrier = pltpu.get_barrier_semaphore()
    for device in [sibling, facing] + [peer_at(ahead(*d)) for d in steps]:
        pl.semaphore_signal(barrier, inc=1, device_id=device, device_id_type=MESH)

    for c in range(chunks_ff):
        weight_copy(0, c).start()
        weight_copy(1, c).start()

    for copy in own:
        copy.wait()
    square = (count_tok, count_tok)
    diagonal = lax.broadcasted_iota(jnp.int32, square, 0) == lax.broadcasted_iota(
        jnp.int32, square, 1
    )

    def column(ref, k):
        line = jnp.broadcast_to(ref[k : k + 1, :].astype(jnp.float32), square)
        return jnp.sum(jnp.where(diagonal, line, 0.0), axis=1, keepdims=True)

    lane = lax.broadcasted_iota(jnp.int32, (count_tok, LANES), 1).astype(jnp.float32)
    marks = jnp.where(lane == column(ids, 0), column(gates, 0), 0.0)
    marks = marks + jnp.where(lane == column(ids, 1), column(gates, 1), 0.0)
    rows_in[core, group, place, :, width : width + LANES] = marks.astype(jnp.bfloat16)

    pl.semaphore_wait(barrier, peers + 1)

    def move(side, of, at, send_sem, device):
        block = rows_in.at[side, of, at]
        return pltpu.make_async_remote_copy(
            src_ref=block,
            dst_ref=block,
            send_sem=send_sem,
            recv_sem=tok_recv.at[side, of, at],
            device_id=device,
            device_id_type=MESH,
        )

    def along_z(dz):
        return move(core, group, place, z_send.at[dz], peer_at(ahead(0, dz)))

    def along_x(dx, dz):
        return move(core, group, behind(0, dz), x_send.at[dx, dz], peer_at(ahead(dx, 0)))

    def along_y(at):
        return move(core, group, at, y_send.at[at], facing)

    def to_sibling(of, at):
        return move(core, of, at, s_send.at[of, at], sibling)

    def landed(side, of, at):
        move(side, of, at, s_send.at[of, at], sibling).wait_recv()

    near = sorted(range(blks), key=lambda dz: min(dz, blks - dz))
    sequence = [(0, dz) for dz in near] + [(dx, dz) for dx in range(1, across) for dz in near]
    for dz in reversed(near):
        if dz:
            along_z(dz).start()
    for i, (dx, dz) in enumerate(sequence):
        at = behind(dx, dz)
        if i:
            landed(core, group, at)
        along_y(at).start()
        if dx == 0:
            for further in range(1, across):
                along_x(further, dz).start()
        to_sibling(group, at).start()
        if i:
            at = behind(*sequence[i - 1])
            landed(core, 1 - group, at)
            to_sibling(1 - group, at).start()
        else:
            for c in range(chunks):
                weight_copy(2, c).start()
    at = behind(*sequence[-1])
    landed(core, 1 - group, at)
    to_sibling(1 - group, at).start()
    for of in range(groups):
        for at in range(peers):
            landed(1 - core, of, at)

    for side in range(2):
        for of in range(groups):
            for at in range(peers):
                first = ((side * groups + of) * peers + at) * count_tok
                rows_f32[first : first + count_tok, :] = rows_in[side, of, at].astype(jnp.float32)
    rows[...] = rows_f32[:, 0:width].astype(jnp.bfloat16)
    marks = rows_f32[:, width : width + LANES]
    lane = lax.broadcasted_iota(jnp.int32, marks.shape, 1)
    share = jnp.sum(jnp.where(lane == expert, marks, 0.0), axis=1, keepdims=True)
    share = share / jnp.sum(marks, axis=1, keepdims=True)

    piece = cols_ff // 2

    def products(p):
        c, first = p // 2, p % 2 * piece
        if first == 0:
            weight_copy(0, c).wait()
            weight_copy(1, c).wait()
        return (
            jnp.dot(rows[...], wg[c, :, first : first + piece], preferred_element_type=jnp.float32),
            jnp.dot(rows[...], wu[c, :, first : first + piece], preferred_element_type=jnp.float32),
        )

    def activate(p, gate_part, up_part):
        value = gate_part / (1.0 + jnp.exp(-gate_part)) * up_part
        hidden[:, p * piece : (p + 1) * piece] = value.astype(jnp.bfloat16)

    held = products(0)
    for p in range(1, 2 * chunks_ff):
        following = products(p)
        activate(p - 1, *held)
        held = following
    activate(2 * chunks_ff - 1, *held)

    def pair(c):
        other = pl.multiple_of((1 - core) * half, half)
        return pltpu.make_async_remote_copy(
            src_ref=part.at[c, pl.ds(other, half), :],
            dst_ref=part_sib.at[c],
            send_sem=sib_send.at[c],
            recv_sem=sib_recv.at[c],
            device_id=sibling,
            device_id_type=MESH,
        )

    def cross(c):
        return pltpu.make_async_remote_copy(
            src_ref=over.at[c],
            dst_ref=over_in.at[c],
            send_sem=over_send.at[c],
            recv_sem=over_recv.at[c],
            device_id=facing,
            device_id_type=MESH,
        )

    def home(c, j):
        at = ahead(*steps[j])
        return pltpu.make_async_remote_copy(
            src_ref=back.at[c, at],
            dst_ref=back_in.at[c, place],
            send_sem=back_send.at[c, j],
            recv_sem=back_recv.at[c, place],
            device_id=peer_at(at),
            device_id_type=MESH,
        )

    def from_peer(c, j):
        at = behind(*steps[j])
        return pltpu.make_async_remote_copy(
            src_ref=back.at[c, at],
            dst_ref=back_in.at[c, at],
            send_sem=back_send.at[c, j],
            recv_sem=back_recv.at[c, at],
            device_id=peer_at(at),
            device_id_type=MESH,
        )

    def pair_sum(c, of):
        mine = pl.multiple_of(core * half + of * quarter, quarter)
        theirs = pl.multiple_of(of * quarter, quarter)
        return part[c, pl.ds(mine, quarter), :] + part_sib[c, pl.ds(theirs, quarter), :]

    def project(c):
        weight_copy(2, c).wait()
        part[c] = jnp.dot(hidden[...], wd[c], preferred_element_type=jnp.float32) * share
        pair(c).start()

    def send_over(c):
        pair(c).wait_recv()
        over[c] = pair_sum(c, 1 - group).astype(jnp.bfloat16)
        cross(c).start()

    def send_home(c):
        kept = pair_sum(c, group)
        cross(c).wait_recv()
        both = kept + over_in[c].astype(jnp.float32)
        for at in range(peers):
            back[c, at] = both[at * count_tok : (at + 1) * count_tok, :].astype(jnp.bfloat16)
        for j in range(peers - 1):
            home(c, j).start()

    for c in range(chunks):
        project(c)
        if c > 1:
            send_over(c - 2)
    for c in range(max(chunks - 2, 0), chunks):
        send_over(c)
        if c > 1:
            send_home(c - 2)
    for c in range(max(chunks - 2, 0), chunks):
        send_home(c)

    for c in range(chunks):
        total = back[c, place].astype(jnp.float32)
        for j in range(peers - 1):
            from_peer(c, j).wait_recv()
            total = total + back_in[c, behind(*steps[j])].astype(jnp.float32)
        out_ref[:, c * cols : (c + 1) * cols] = total

    for dz in range(blks):
        if dz:
            along_z(dz).wait_send()
        for dx in range(1, across):
            along_x(dx, dz).wait_send()
    for at in range(peers):
        along_y(at).wait_send()
        for of in range(groups):
            to_sibling(of, at).wait_send()
    for c in range(chunks):
        pair(c).wait_send()
        cross(c).wait_send()
        for j in range(peers - 1):
            home(c, j).wait_send()


def dense(tokens, route_ids, route_slots, gate_fixed, w_gate, w_up, w_down):
    count_tok, width = tokens.shape
    groups, experts, blks = (lax.axis_size(name) for name in ("group", "expert", "blk"))
    units = w_gate.shape[2] // groups
    peers = experts // 2 * blks
    quarter = peers * count_tok
    half = groups * quarter
    rows_all = 2 * half
    cols, cols_ff = width // CHUNKS, units // CHUNKS_FF
    f32, bf16 = jnp.float32, jnp.bfloat16
    dma = pltpu.SemaphoreType.DMA
    total = pl.pallas_call(
        functools.partial(kernel, groups, experts, blks),
        out_shape=jax.ShapeDtypeStruct((count_tok, width), f32),
        in_specs=[pl.BlockSpec(memory_space=pltpu.HBM)] * 6,
        out_specs=pl.BlockSpec(memory_space=pltpu.VMEM),
        scratch_shapes=[
            pltpu.VMEM((2, count_tok), jnp.int32),
            pltpu.VMEM((2, count_tok), jnp.int32),
            pltpu.VMEM((CHUNKS_FF, width, cols_ff), bf16),
            pltpu.VMEM((CHUNKS_FF, width, cols_ff), bf16),
            pltpu.VMEM((CHUNKS, units, cols), bf16),
            pltpu.VMEM((2, groups, peers, count_tok, width + LANES), bf16),
            pltpu.VMEM((rows_all, width + LANES), f32),
            pltpu.VMEM((rows_all, width), bf16),
            pltpu.VMEM((rows_all, units), bf16),
            pltpu.VMEM((CHUNKS, rows_all, cols), f32),
            pltpu.VMEM((CHUNKS, half, cols), f32),
            pltpu.VMEM((CHUNKS, quarter, cols), bf16),
            pltpu.VMEM((CHUNKS, quarter, cols), bf16),
            pltpu.VMEM((CHUNKS, peers, count_tok, cols), bf16),
            pltpu.VMEM((CHUNKS, peers, count_tok, cols), bf16),
            dma((3,)),
            dma((3, max(CHUNKS, CHUNKS_FF))),
            dma((blks,)),
            dma((max(experts // 2, 1), blks)),
            dma((peers,)),
            dma((groups, peers)),
            dma((2, groups, peers)),
            dma((CHUNKS,)),
            dma((CHUNKS,)),
            dma((CHUNKS,)),
            dma((CHUNKS,)),
            dma((CHUNKS, peers)),
            dma((CHUNKS, peers)),
        ],
        compiler_params=pltpu.CompilerParams(
            collective_id=0, has_side_effects=True, vmem_limit_bytes=63 * 1024 * 1024
        ),
        cost_estimate=pl.CostEstimate(
            flops=6 * rows_all * width * units,
            bytes_accessed=6 * width * units,
            transcendentals=rows_all * units,
        ),
    )(tokens, route_ids.T, gate_fixed.T, w_gate, w_up, w_down)
    return total.astype(bf16)


def on_device(tokens, *others):
    count_tok = tokens.shape[0]
    groups, experts = lax.axis_size("group"), lax.axis_size("expert")
    whole = 4 * count_tok // experts >= count_tok and experts % 2 == 0 and experts <= LANES
    return (dense if whole and groups == 2 else routed)(tokens, *others)


def solution(mesh):
    return jax.shard_map(
        on_device,
        mesh=mesh,
        in_specs=(
            P(("group", "expert", "blk"), None),
            P(("group", "expert", "blk"), None),
            P(("group", "expert", "blk"), None),
            P(("group", "expert", "blk"), None),
            P("expert", None, "blk"),
            P("expert", None, "blk"),
            P("expert", "blk", None),
        ),
        out_specs=P(("group", "expert", "blk"), None),
        check_vma=False,
    )
```

time: 26 us -> 36.8 us (1.42)
  Pallas kernels: 24.3 us -> 35.2 us
  other arithmetic: 0 us -> 1.37 us
  local copies, waits for them, and re-layouts: 1.33 us -> 0 us
    pallas_call x1, Pallas kernels: 24.3 us -> 35.2 us  [dense(): pl.pallas_call(functools.partial(kernel, groups, experts, blks), out_shap...]
    convert_element_type x0 -> x1, other arithmetic: none -> 1.37 us  [dense(): return total.astype(bf16)]
    unnamed x1 -> x0, local copies, waits for them, and re-layouts: 1.33 us -> none
where the time goes in v3:
time: 36.8 us; the launch traced here: 36.6 us
  Pallas kernels  35.2 us (96%)
  other arithmetic  1.37 us (4%)
    pallas_call x1, Pallas kernels, dense(): pl.pallas_call(functools.partial(kernel, groups, experts, blks), out_shap...  35.2 us
    convert_element_type x1, other arithmetic, dense(): return total.astype(bf16)  1.37 us

profile of v3, /device:TPU:0, one launch (start us, length us, event | category | flops | bytes accessed | tf_op | source)
XLA Modules:
  0.0 36.6 jit_solution(13242597006719674453)
XLA Ops:
  0.0 35.2 %shard_map.64 = f32[4,2048]{1,0:T(4,128)} custom-call(bf16[4,2048]{1,0:T(4,128)(2,1)} %tok_hbm.1, s32[2,4]{1,0:T(2,128)} %bitcast.2, s32[2,4]{1,0:T(2,128)} %bitcast.3, bf16[1,2048,2048]{2,1,0:T(8,128)(2,1)} %wg_hbm.1, bf16[1,2048,2048]{2,1,0:T(8,128)(2,1)} %wu_hbm.1, bf16[1,2048,2048]{2,1,0:T(8,128)(2,1)} %wd_hbm.1), custom_call_target="tpu_custom_call" | custom-call | flops 1610612736 | bytes 12582912 | tf_op jit(solution)/shard_map/pallas_call | solution.py:337
  35.2 1.4 %convert_element_type.3 = bf16[4,2048]{1,0:T(4,128)(2,1)} convert(f32[4,2048]{1,0:T(4,128)} %shard_map.64) | non-fusion elementwise | flops 8192 | bytes 49152 | tf_op jit(solution)/shard_map/convert_element_type | solution.py:381

commit v4 on v2

--- a/solution.py
+++ b/solution.py
@@ -9,6 +9,7 @@
 
 MESH = pl.DeviceIdType.MESH
 CHUNKS = 4
+ROW_CHUNKS = 4
 LANES = 128
 
 
@@ -55,15 +56,15 @@
 
 def kernel(
     experts, blks, tok_hbm, ids_hbm, gate_hbm, wg_hbm, wu_hbm, wd_hbm, out_ref,
-    ids, gates, wg, wu, wd, rows_in, rows_f32, rows, hidden, part, part_sib, back, back_in,
+    ids, gates, wg, wu, wd, rows_in, rows_f32, rows, hidden, part, part_out, part_sib, back, back_in,
     in_sem, w_sem, tok_send, tok_fwd, tok_recv, sib_send, sib_recv, back_send, back_recv,
 ):
     count_tok, width = tok_hbm.shape
     across = experts // 2
     peers = across * blks
     half = peers * count_tok
-    chunks_ff, unused, cols_ff = wg.shape
-    chunks, unused, cols = wd.shape
+    units = wg.shape[1]
+    chunks, unused, cols = part.shape
     expert, blk = lax.axis_index("expert"), lax.axis_index("blk")
     core = lax.rem(expert, 2)
     place = expert // 2 * blks + blk
@@ -87,10 +88,9 @@
 
     def weight_copy(mat, c):
         hbm, vmem = ((wg_hbm, wg), (wu_hbm, wu), (wd_hbm, wd))[mat]
-        n = vmem.shape[2]
-        return pltpu.make_async_copy(
-            hbm.at[0, :, pl.ds(pl.multiple_of(c * n, n), n)], vmem.at[c], w_sem.at[mat, c]
-        )
+        n = vmem.shape[0] // ROW_CHUNKS
+        stretch = pl.ds(c * n, n)
+        return pltpu.make_async_copy(hbm.at[0, stretch, :], vmem.at[stretch, :], w_sem.at[mat, c])
 
     own = [
         pltpu.make_async_copy(ids_hbm, ids, in_sem.at[0]),
@@ -101,10 +101,6 @@
     ]
     for copy in own:
         copy.start()
-    for c in range(chunks_ff // 2):
-        weight_copy(0, c).start()
-        weight_copy(1, c).start()
-
     barrier = pltpu.get_barrier_semaphore()
     pl.semaphore_signal(barrier, inc=1, device_id=sibling, device_id_type=MESH)
     for j in range(peers - 1):
@@ -112,6 +108,9 @@
             barrier, inc=1, device_id=peer_at(ahead(j)), device_id_type=MESH
         )
 
+    for mat in range(3):
+        for c in range(ROW_CHUNKS):
+            weight_copy(mat, c).start()
     for copy in own:
         copy.wait()
     square = (count_tok, count_tok)
@@ -153,18 +152,12 @@
     for j in range(peers - 1):
         to_peer(j).start()
     arrival(core, place).start()
-    for c in range(chunks_ff // 2, chunks_ff):
-        weight_copy(0, c).start()
-        weight_copy(1, c).start()
     for j in reversed(range(peers - 1)):
         at = behind(j)
         arrival(core, at).wait_recv()
         arrival(core, at).start()
-    for c in range(chunks):
-        weight_copy(2, c).start()
     for j in range(peers):
         arrival(1 - core, j).wait_recv()
-
     for side in range(2):
         for at in range(peers):
             first = (side * peers + at) * count_tok
@@ -175,30 +168,34 @@
     share = jnp.sum(jnp.where(lane == expert, marks, 0.0), axis=1, keepdims=True)
     share = share / jnp.sum(marks, axis=1, keepdims=True)
 
-    def products(c):
-        weight_copy(0, c).wait()
-        weight_copy(1, c).wait()
+    piece = units // chunks
+
+    def products(p):
+        columns = slice(p * piece, (p + 1) * piece)
         return (
-            jnp.dot(rows[...], wg[c], preferred_element_type=jnp.float32),
-            jnp.dot(rows[...], wu[c], preferred_element_type=jnp.float32),
-        )
-
-    def activate(c, gate_part, up_part):
+            jnp.dot(rows[...], wg[:, columns], preferred_element_type=jnp.float32),
+            jnp.dot(rows[...], wu[:, columns], preferred_element_type=jnp.float32),
+        )
+
+    def activate(p, gate_part, up_part):
         value = gate_part / (1.0 + jnp.exp(-gate_part)) * up_part
-        hidden[:, c * cols_ff : (c + 1) * cols_ff] = value.astype(jnp.bfloat16)
-
+        hidden[:, p * piece : (p + 1) * piece] = value.astype(jnp.bfloat16)
+
+    for mat in range(2):
+        for c in range(ROW_CHUNKS):
+            weight_copy(mat, c).wait()
     held = products(0)
-    for c in range(1, chunks_ff):
-        following = products(c)
-        activate(c - 1, *held)
+    for p in range(1, chunks):
+        following = products(p)
+        activate(p - 1, *held)
         held = following
-    activate(chunks_ff - 1, *held)
+    activate(chunks - 1, *held)
+    for c in range(ROW_CHUNKS):
+        weight_copy(2, c).wait()
 
     def pair(c):
-        mine = pl.multiple_of(core * half, half)
-        other = pl.multiple_of((1 - core) * half, half)
-        return mine, pltpu.make_async_remote_copy(
-            src_ref=part.at[c, pl.ds(other, half), :],
+        return pltpu.make_async_remote_copy(
+            src_ref=part_out.at[c],
             dst_ref=part_sib.at[c],
             send_sem=sib_send.at[c],
             recv_sem=sib_recv.at[c],
@@ -229,18 +226,20 @@
         )
 
     def send_home(c):
-        mine, copy = pair(c)
-        copy.wait_recv()
-        both = part[c, pl.ds(mine, half), :] + part_sib[c]
+        mine = pl.multiple_of(core * half, half)
+        pair(c).wait_recv()
+        both = part[c, pl.ds(mine, half), :] + part_sib[c].astype(jnp.float32)
         for at in range(peers):
             back[c, at] = both[at * count_tok : (at + 1) * count_tok, :].astype(jnp.bfloat16)
         for j in range(peers - 1):
             home(c, j).start()
 
     for c in range(chunks):
-        weight_copy(2, c).wait()
-        part[c] = jnp.dot(hidden[...], wd[c], preferred_element_type=jnp.float32) * share
-        pair(c)[1].start()
+        columns = slice(c * cols, (c + 1) * cols)
+        part[c] = jnp.dot(hidden[...], wd[:, columns], preferred_element_type=jnp.float32) * share
+        other = pl.multiple_of((1 - core) * half, half)
+        part_out[c] = part[c, pl.ds(other, half), :].astype(jnp.bfloat16)
+        pair(c).start()
         if c > 0:
             send_home(c - 1)
     send_home(chunks - 1)
@@ -257,7 +256,7 @@
         to_peer(j).wait_send()
         arrival(core, behind(j)).wait_send()
     for c in range(chunks):
-        pair(c)[1].wait_send()
+        pair(c).wait_send()
         for j in range(peers - 1):
             home(c, j).wait_send()
 
@@ -269,7 +268,7 @@
     peers = experts // 2 * blks
     half = peers * count_tok
     rows_all = 2 * half
-    cols, cols_ff = width // CHUNKS, units // CHUNKS
+    cols = width // CHUNKS
     f32, bf16 = jnp.float32, jnp.bfloat16
     dma = pltpu.SemaphoreType.DMA
     return pl.pallas_call(
@@ -280,19 +279,20 @@
         scratch_shapes=[
             pltpu.VMEM((2, count_tok), jnp.int32),
             pltpu.VMEM((2, count_tok), jnp.int32),
-            pltpu.VMEM((CHUNKS, width, cols_ff), bf16),
-            pltpu.VMEM((CHUNKS, width, cols_ff), bf16),
-            pltpu.VMEM((CHUNKS, units, cols), bf16),
+            pltpu.VMEM((width, units), bf16),
+            pltpu.VMEM((width, units), bf16),
+            pltpu.VMEM((units, width), bf16),
             pltpu.VMEM((2, peers, count_tok, width + LANES), bf16),
             pltpu.VMEM((rows_all, width + LANES), f32),
             pltpu.VMEM((rows_all, width), bf16),
             pltpu.VMEM((rows_all, units), bf16),
             pltpu.VMEM((CHUNKS, rows_all, cols), f32),
-            pltpu.VMEM((CHUNKS, half, cols), f32),
+            pltpu.VMEM((CHUNKS, half, cols), bf16),
+            pltpu.VMEM((CHUNKS, half, cols), bf16),
             pltpu.VMEM((CHUNKS, peers, count_tok, cols), bf16),
             pltpu.VMEM((CHUNKS, peers, count_tok, cols), bf16),
             dma((3,)),
-            dma((3, CHUNKS)),
+            dma((3, ROW_CHUNKS)),
             dma((peers,)),
             dma((peers,)),
             dma((2, peers)),

time: 26 us -> 25.4 us (0.977)
  Pallas kernels: 24.3 us -> 23.8 us
    pallas_call x1, Pallas kernels: 24.3 us -> 23.8 us  [dense(): pl.pallas_call(functools.partial(kernel, experts, blks), out_shape=jax.Sh...]
where the time goes in v4:
time: 25.4 us; the launch traced here: 25.1 us
  Pallas kernels  23.8 us (94%)
  local copies, waits for them, and re-layouts  1.33 us (5%)
    pallas_call x1, Pallas kernels, dense(): pl.pallas_call(functools.partial(kernel, experts, blks), out_shape=jax.Sh...  23.8 us
    unnamed x1, local copies, waits for them, and re-layouts  1.33 us

profile of v4, /device:TPU:0, one launch (start us, length us, event | category | flops | bytes accessed | tf_op | source)
XLA Modules:
  0.0 25.1 jit_solution(13428972518866750222)
XLA Ops:
  0.0 23.8 %shard_map.64 = bf16[4,2048]{1,0:T(4,128)(2,1)} custom-call(bf16[4,2048]{1,0:T(4,128)(2,1)} %tok_hbm.1, s32[2,4]{1,0:T(2,128)} %bitcast.2, s32[2,4]{1,0:T(2,128)} %bitcast.3, bf16[1,2048,2048]{2,1,0:T(8,128)(2,1)} %wg_hbm.1, bf16[1,2048,2048]{2,1,0:T(8,128)(2,1)} %wu_hbm.1, bf16[1,2048,2048]{2,1,0:T(8,128)(2,1)} %wd_hbm.1), custom_call_target="tpu_custom_call" | custom-call | flops 1610612736 | bytes 25165824 | tf_op jit(solution)/shard_map/pallas_call | solution.py:274
  23.8 1.3 %copy.8 = bf16[4,2048]{1,0:T(4,128)(2,1)} copy(bf16[4,2048]{1,0:T(4,128)(2,1)} %shard_map.64) | data formatting | bytes 32768

commit v5 on v4

--- a/solution.py
+++ b/solution.py
@@ -10,6 +10,7 @@
 MESH = pl.DeviceIdType.MESH
 CHUNKS = 4
 ROW_CHUNKS = 4
+DEPTH = 256
 LANES = 128
 
 
@@ -96,7 +97,7 @@
         pltpu.make_async_copy(ids_hbm, ids, in_sem.at[0]),
         pltpu.make_async_copy(gate_hbm, gates, in_sem.at[1]),
         pltpu.make_async_copy(
-            tok_hbm, rows_in.at[core, place, :, pl.ds(0, width)], in_sem.at[2]
+            tok_hbm, rows_in.at[0, place, :, pl.ds(0, width)], in_sem.at[2]
         ),
     ]
     for copy in own:
@@ -125,43 +126,56 @@
     lane = lax.broadcasted_iota(jnp.int32, (count_tok, LANES), 1).astype(jnp.float32)
     marks = jnp.where(lane == column(ids, 0), column(gates, 0), 0.0)
     marks = marks + jnp.where(lane == column(ids, 1), column(gates, 1), 0.0)
-    rows_in[core, place, :, width : width + LANES] = marks.astype(jnp.bfloat16)
+    rows_in[0, place, :, width : width + LANES] = marks.astype(jnp.bfloat16)
 
     pl.semaphore_wait(barrier, peers)
 
     def to_peer(j):
         return pltpu.make_async_remote_copy(
-            src_ref=rows_in.at[core, place],
-            dst_ref=rows_in.at[core, place],
+            src_ref=rows_in.at[0, place],
+            dst_ref=rows_in.at[0, place],
             send_sem=tok_send.at[j],
-            recv_sem=tok_recv.at[core, place],
+            recv_sem=tok_recv.at[0, place],
             device_id=peer_at(ahead(j)),
             device_id_type=MESH,
         )
 
-    def arrival(side, at):
-        return pltpu.make_async_remote_copy(
+    def to_sibling(at):
+        return pltpu.make_async_remote_copy(
+            src_ref=rows_in.at[0, at],
+            dst_ref=rows_in.at[1, at],
+            send_sem=tok_fwd.at[at],
+            recv_sem=tok_recv.at[1, at],
+            device_id=sibling,
+            device_id_type=MESH,
+        )
+
+    def landed(side, at):
+        pltpu.make_async_remote_copy(
             src_ref=rows_in.at[side, at],
             dst_ref=rows_in.at[side, at],
             send_sem=tok_fwd.at[at],
             recv_sem=tok_recv.at[side, at],
             device_id=sibling,
             device_id_type=MESH,
-        )
-
-    for j in range(peers - 1):
-        to_peer(j).start()
-    arrival(core, place).start()
-    for j in reversed(range(peers - 1)):
-        at = behind(j)
-        arrival(core, at).wait_recv()
-        arrival(core, at).start()
-    for j in range(peers):
-        arrival(1 - core, j).wait_recv()
-    for side in range(2):
+        ).wait_recv()
+
+    def unpack(side):
         for at in range(peers):
             first = (side * peers + at) * count_tok
             rows_f32[first : first + count_tok, :] = rows_in[side, at].astype(jnp.float32)
+
+    for j in range(peers - 1):
+        to_peer(j).start()
+    to_sibling(place).start()
+    for j in reversed(range(peers - 1)):
+        at = behind(j)
+        landed(0, at)
+        to_sibling(at).start()
+    unpack(0)
+    for at in range(peers):
+        landed(1, at)
+    unpack(1)
     rows[...] = rows_f32[:, 0:width].astype(jnp.bfloat16)
     marks = rows_f32[:, width : width + LANES]
     lane = lax.broadcasted_iota(jnp.int32, marks.shape, 1)
@@ -170,12 +184,17 @@
 
     piece = units // chunks
 
+    def times(left, mat, columns):
+        total = None
+        for k in range(0, left.shape[1], DEPTH):
+            deep = slice(k, k + DEPTH)
+            term = jnp.dot(left[:, deep], mat[deep, columns], preferred_element_type=jnp.float32)
+            total = term if total is None else total + term
+        return total
+
     def products(p):
         columns = slice(p * piece, (p + 1) * piece)
-        return (
-            jnp.dot(rows[...], wg[:, columns], preferred_element_type=jnp.float32),
-            jnp.dot(rows[...], wu[:, columns], preferred_element_type=jnp.float32),
-        )
+        return times(rows, wg, columns), times(rows, wu, columns)
 
     def activate(p, gate_part, up_part):
         value = gate_part / (1.0 + jnp.exp(-gate_part)) * up_part
@@ -226,9 +245,8 @@
         )
 
     def send_home(c):
-        mine = pl.multiple_of(core * half, half)
         pair(c).wait_recv()
-        both = part[c, pl.ds(mine, half), :] + part_sib[c].astype(jnp.float32)
+        both = part[c] + part_sib[c].astype(jnp.float32)
         for at in range(peers):
             back[c, at] = both[at * count_tok : (at + 1) * count_tok, :].astype(jnp.bfloat16)
         for j in range(peers - 1):
@@ -236,9 +254,9 @@
 
     for c in range(chunks):
         columns = slice(c * cols, (c + 1) * cols)
-        part[c] = jnp.dot(hidden[...], wd[:, columns], preferred_element_type=jnp.float32) * share
-        other = pl.multiple_of((1 - core) * half, half)
-        part_out[c] = part[c, pl.ds(other, half), :].astype(jnp.bfloat16)
+        scaled = times(hidden, wd, columns) * share
+        part[c] = scaled[0:half, :]
+        part_out[c] = scaled[half:, :].astype(jnp.bfloat16)
         pair(c).start()
         if c > 0:
             send_home(c - 1)
@@ -251,10 +269,10 @@
             total = total + back_in[c, behind(j)].astype(jnp.float32)
         out_ref[:, c * cols : (c + 1) * cols] = total.astype(jnp.bfloat16)
 
-    arrival(core, place).wait_send()
     for j in range(peers - 1):
         to_peer(j).wait_send()
-        arrival(core, behind(j)).wait_send()
+    for at in range(peers):
+        to_sibling(at).wait_send()
     for c in range(chunks):
         pair(c).wait_send()
         for j in range(peers - 1):
@@ -286,7 +304,7 @@
             pltpu.VMEM((rows_all, width + LANES), f32),
             pltpu.VMEM((rows_all, width), bf16),
             pltpu.VMEM((rows_all, units), bf16),
-            pltpu.VMEM((CHUNKS, rows_all, cols), f32),
+            pltpu.VMEM((CHUNKS, half, cols), f32),
             pltpu.VMEM((CHUNKS, half, cols), bf16),
             pltpu.VMEM((CHUNKS, half, cols), bf16),
             pltpu.VMEM((CHUNKS, peers, count_tok, cols), bf16),

time: 25.4 us -> 25.3 us (level)
  no operation moved by 1% of the time
where the time goes in v5:
time: 25.3 us; the launch traced here: 25.1 us
  Pallas kernels  23.8 us (94%)
  local copies, waits for them, and re-layouts  1.33 us (5%)
    pallas_call x1, Pallas kernels, dense(): pl.pallas_call(functools.partial(kernel, experts, blks), out_shape=jax.Sh...  23.8 us
    unnamed x1, local copies, waits for them, and re-layouts  1.33 us

profile of v5, /device:TPU:0, one launch (start us, length us, event | category | flops | bytes accessed | tf_op | source)
XLA Modules:
  0.0 25.1 jit_solution(12242877915649382854)
XLA Ops:
  0.0 23.8 %shard_map.64 = bf16[4,2048]{1,0:T(4,128)(2,1)} custom-call(bf16[4,2048]{1,0:T(4,128)(2,1)} %tok_hbm.1, s32[2,4]{1,0:T(2,128)} %bitcast.2, s32[2,4]{1,0:T(2,128)} %bitcast.3, bf16[1,2048,2048]{2,1,0:T(8,128)(2,1)} %wg_hbm.1, bf16[1,2048,2048]{2,1,0:T(8,128)(2,1)} %wu_hbm.1, bf16[1,2048,2048]{2,1,0:T(8,128)(2,1)} %wd_hbm.1), custom_call_target="tpu_custom_call" | custom-call | flops 1610612736 | bytes 25165824 | tf_op jit(solution)/shard_map/pallas_call | solution.py:292
  23.8 1.3 %copy.8 = bf16[4,2048]{1,0:T(4,128)(2,1)} copy(bf16[4,2048]{1,0:T(4,128)(2,1)} %shard_map.64) | data formatting | bytes 32768

commit v6 on v5

--- a/solution.py
+++ b/solution.py
@@ -258,9 +258,10 @@
         part[c] = scaled[0:half, :]
         part_out[c] = scaled[half:, :].astype(jnp.bfloat16)
         pair(c).start()
-        if c > 0:
-            send_home(c - 1)
-    send_home(chunks - 1)
+        if c > 1:
+            send_home(c - 2)
+    for c in range(max(chunks - 2, 0), chunks):
+        send_home(c)
 
     for c in range(chunks):
         total = back[c, place].astype(jnp.float32)

time: 25.3 us -> 25.2 us (level)
  no operation moved by 1% of the time
where the time goes in v6:
time: 25.2 us; the launch traced here: 25 us
  Pallas kernels  23.6 us (94%)
  local copies, waits for them, and re-layouts  1.33 us (5%)
    pallas_call x1, Pallas kernels, dense(): pl.pallas_call(functools.partial(kernel, experts, blks), out_shape=jax.Sh...  23.6 us
    unnamed x1, local copies, waits for them, and re-layouts  1.33 us

profile of v6, /device:TPU:0, one launch (start us, length us, event | category | flops | bytes accessed | tf_op | source)
XLA Modules:
  0.0 25.0 jit_solution(5712769077378534000)
XLA Ops:
  0.0 23.6 %shard_map.64 = bf16[4,2048]{1,0:T(4,128)(2,1)} custom-call(bf16[4,2048]{1,0:T(4,128)(2,1)} %tok_hbm.1, s32[2,4]{1,0:T(2,128)} %bitcast.2, s32[2,4]{1,0:T(2,128)} %bitcast.3, bf16[1,2048,2048]{2,1,0:T(8,128)(2,1)} %wg_hbm.1, bf16[1,2048,2048]{2,1,0:T(8,128)(2,1)} %wu_hbm.1, bf16[1,2048,2048]{2,1,0:T(8,128)(2,1)} %wd_hbm.1), custom_call_target="tpu_custom_call" | custom-call | flops 1610612736 | bytes 25165824 | tf_op jit(solution)/shard_map/pallas_call | solution.py:293
  23.6 1.3 %copy.8 = bf16[4,2048]{1,0:T(4,128)(2,1)} copy(bf16[4,2048]{1,0:T(4,128)(2,1)} %shard_map.64) | data formatting | bytes 32768

commit v7 on v6

--- a/solution.py
+++ b/solution.py
@@ -160,23 +160,29 @@
             device_id_type=MESH,
         ).wait_recv()
 
-    def unpack(side):
-        for at in range(peers):
-            first = (side * peers + at) * count_tok
-            rows_f32[first : first + count_tok, :] = rows_in[side, at].astype(jnp.float32)
+    order = [place] + [behind(j) for j in reversed(range(peers - 1))]
+
+    def unpack(side, i):
+        first = (side * peers + i) * count_tok
+        rows_f32[first : first + count_tok, :] = rows_in[side, order[i]].astype(jnp.float32)
+
+    def finish(side):
+        rows[side * half : (side + 1) * half, :] = rows_f32[
+            side * half : (side + 1) * half, 0:width
+        ].astype(jnp.bfloat16)
 
     for j in range(peers - 1):
         to_peer(j).start()
-    to_sibling(place).start()
-    for j in reversed(range(peers - 1)):
-        at = behind(j)
-        landed(0, at)
+    for i, at in enumerate(order):
+        if i:
+            landed(0, at)
         to_sibling(at).start()
-    unpack(0)
-    for at in range(peers):
+        unpack(0, i)
+    finish(0)
+    for i, at in enumerate(order):
         landed(1, at)
-    unpack(1)
-    rows[...] = rows_f32[:, 0:width].astype(jnp.bfloat16)
+        unpack(1, i)
+    finish(1)
     marks = rows_f32[:, width : width + LANES]
     lane = lax.broadcasted_iota(jnp.int32, marks.shape, 1)
     share = jnp.sum(jnp.where(lane == expert, marks, 0.0), axis=1, keepdims=True)
@@ -222,25 +228,23 @@
             device_id_type=MESH,
         )
 
-    def home(c, j):
-        at = ahead(j)
-        return pltpu.make_async_remote_copy(
-            src_ref=back.at[c, at],
+    def home(c, i):
+        return pltpu.make_async_remote_copy(
+            src_ref=back.at[c, i],
             dst_ref=back_in.at[c, place],
-            send_sem=back_send.at[c, j],
+            send_sem=back_send.at[c, i],
             recv_sem=back_recv.at[c, place],
-            device_id=peer_at(at),
-            device_id_type=MESH,
-        )
-
-    def from_peer(c, j):
-        at = behind(j)
-        return pltpu.make_async_remote_copy(
-            src_ref=back.at[c, at],
-            dst_ref=back_in.at[c, at],
-            send_sem=back_send.at[c, j],
-            recv_sem=back_recv.at[c, at],
-            device_id=peer_at(at),
+            device_id=peer_at(order[i]),
+            device_id_type=MESH,
+        )
+
+    def from_peer(c, i):
+        return pltpu.make_async_remote_copy(
+            src_ref=back.at[c, i],
+            dst_ref=back_in.at[c, order[i]],
+            send_sem=back_send.at[c, i],
+            recv_sem=back_recv.at[c, order[i]],
+            device_id=peer_at(order[i]),
             device_id_type=MESH,
         )
 
@@ -249,8 +253,8 @@
         both = part[c] + part_sib[c].astype(jnp.float32)
         for at in range(peers):
             back[c, at] = both[at * count_tok : (at + 1) * count_tok, :].astype(jnp.bfloat16)
-        for j in range(peers - 1):
-            home(c, j).start()
+        for i in reversed(range(1, peers)):
+            home(c, i).start()
 
     for c in range(chunks):
         columns = slice(c * cols, (c + 1) * cols)
@@ -264,10 +268,10 @@
         send_home(c)
 
     for c in range(chunks):
-        total = back[c, place].astype(jnp.float32)
-        for j in range(peers - 1):
-            from_peer(c, j).wait_recv()
-            total = total + back_in[c, behind(j)].astype(jnp.float32)
+        total = back[c, 0].astype(jnp.float32)
+        for i in range(1, peers):
+            from_peer(c, i).wait_recv()
+            total = total + back_in[c, order[i]].astype(jnp.float32)
         out_ref[:, c * cols : (c + 1) * cols] = total.astype(jnp.bfloat16)
 
     for j in range(peers - 1):
@@ -276,8 +280,8 @@
         to_sibling(at).wait_send()
     for c in range(chunks):
         pair(c).wait_send()
-        for j in range(peers - 1):
-            home(c, j).wait_send()
+        for i in range(1, peers):
+            home(c, i).wait_send()
 
 
 def dense(tokens, route_ids, route_slots, gate_fixed, w_gate, w_up, w_down):

time: 25.2 us -> 25.2 us (level)
  no operation moved by 1% of the time
where the time goes in v7:
time: 25.2 us; the launch traced here: 25 us
  Pallas kernels  23.6 us (94%)
  local copies, waits for them, and re-layouts  1.33 us (5%)
    pallas_call x1, Pallas kernels, dense(): pl.pallas_call(functools.partial(kernel, experts, blks), out_shape=jax.Sh...  23.6 us
    unnamed x1, local copies, waits for them, and re-layouts  1.33 us

profile of v7, /device:TPU:0, one launch (start us, length us, event | category | flops | bytes accessed | tf_op | source)
XLA Modules:
  0.0 25.0 jit_solution(974145071599086959)
XLA Ops:
  0.0 23.6 %shard_map.64 = bf16[4,2048]{1,0:T(4,128)(2,1)} custom-call(bf16[4,2048]{1,0:T(4,128)(2,1)} %tok_hbm.1, s32[2,4]{1,0:T(2,128)} %bitcast.2, s32[2,4]{1,0:T(2,128)} %bitcast.3, bf16[1,2048,2048]{2,1,0:T(8,128)(2,1)} %wg_hbm.1, bf16[1,2048,2048]{2,1,0:T(8,128)(2,1)} %wu_hbm.1, bf16[1,2048,2048]{2,1,0:T(8,128)(2,1)} %wd_hbm.1), custom_call_target="tpu_custom_call" | custom-call | flops 1610612736 | bytes 25165824 | tf_op jit(solution)/shard_map/pallas_call | solution.py:297
  23.6 1.3 %copy.8 = bf16[4,2048]{1,0:T(4,128)(2,1)} copy(bf16[4,2048]{1,0:T(4,128)(2,1)} %shard_map.64) | data formatting | bytes 32768
